TPU v7x, 128 devices: a whole 4x4x4 slice. The times are simulated.
128 devices in a mesh: lon: 16 (over y, x_hi, core), lat: 8 (over x_lo, z).
Axes of the slice: x: 4 (x_hi: 2, x_lo: 2; x = x_hi * 2 + x_lo), y: 4, z: 4, core: 2. Of those that a mesh axis runs over, the one named last changes fastest.
Arguments:
- tracers: float32 [6, 24, 512, 2048], P(None, None, 'lat', 'lon'), may hold values from -6 to 6
- flow_east: float32 [24, 512, 2048], P(None, 'lat', 'lon'), may hold values from -0.35 to 0.35
- flow_north: float32 [24, 512, 2048], P(None, 'lat', 'lon'), may hold values from -0.35 to 0.35
- sea_mask: int32 [24, 512, 2048], P(None, 'lat', 'lon'), may hold values 0 or 1
- atm_fields: bfloat16 [4, 1048576], P(None, ('lon', 'lat')), may hold values from -6 to 6
- remap_weights: bfloat16 [32768, 128, 128], P(('lon', 'lat')), may hold values from -0.5 to 0.5
- remap_src: int32 [32768], P(('lon', 'lat')), may hold values from 0 to 63
- remap_dst: int32 [32768], P(('lon', 'lat')), may hold values from 0 to 8191, as said below
- fold_partner: int32 [2048], P('lon'), may hold values from 0 to 2047, as said below
Outputs:
- forcing: float32 [4, 512, 2048], P(None, 'lat', 'lon')
- tracers_next: float32 [6, 24, 512, 2048], P(None, None, 'lat', 'lon')
Inputs may be any that keep to these rules, and one draw needn't show every extreme that they name: `remap_dst`: the weight blocks held by one device name at most 4 destination blocks on any one device; in every draw one device is named 4 times by the blocks of every device. fold_partner[i] = (c - i) mod 2048 for one c.
All inputs are finite; a program needn't handle non-finite values. No bound on the sum of `sea_mask` on one device may be relied on, other than what follows from the above.
Results may differ from a plain program's by a relative error of at most 0.0003.
Values sent between devices are 32-bit elements; how exact they have to be, the bound alone decides.
No kernel may reach another device: no remote copies, remote signals or barrier semaphores. Data moves between devices by JAX's collectives and lax.ppermute only.
A program may use at most 192 MiB of HBM per device.

v0:
```python
import functools

import jax
import jax.numpy as jnp
from jax import lax
from jax.experimental import pallas as pl
from jax.experimental.pallas import tpu as pltpu
from jax.sharding import PartitionSpec as P

HEAT_SCALE = 0.1
FRESH_SCALE = 0.03
STRESS_SCALE = 0.02
HEAT_ALPHA_COEFF = 0.2
SALT_BETA_COEFF = 0.8
SLOPE_EPS = 0.5
DIFFUSIVITY = 0.1

NTR = 6
ROWS = 64
LANES = 128
GROUPS = 8
F32 = jnp.float32
VMEM_LIMIT = 56 * 1024 * 1024


def roll(x, shift):
    return pltpu.roll(x, shift % LANES, axis=1)


def lanes_of(shape):
    return lax.broadcasted_iota(jnp.int32, shape, len(shape) - 1)


def pack_kernel(tracers, east, north, mask, both_ref, cols_ref, up_ref, down_ref):
    lane_group = lanes_of((8, LANES)) // 4
    levels = east.shape[0]
    for k in range(levels):
        land = mask[k].astype(F32)
        fields = [tracers[t, k] for t in range(NTR)] + [east[k], land]
        for h in range(2):
            total = jnp.zeros((8, LANES), F32)
            for rr in range(4):
                start = (4 * h + rr) * 8
                for f in range(8):
                    moved = roll(fields[f][start : start + 8], 2 + 32 * rr + 4 * f)
                    total = jnp.where(lane_group == 8 * rr + f, moved, total)
            both_ref[k, h] = total
            cols_ref[k, h] = total
        fields[6] = north[k]
        for f in range(8):
            both_ref[k, 2, f : f + 1] = fields[f][ROWS - 1 : ROWS]
            for i in range(2):
                up_ref[k, i, f : f + 1] = fields[f][ROWS - 2 + i : ROWS - 1 + i]
                down_ref[k, i, f : f + 1] = fields[f][i : i + 1]


def pack_halos(tracers, east, north, mask):
    levels = east.shape[0]
    step = 2
    flow = pl.BlockSpec((step, ROWS, LANES), lambda i: (i, 0, 0))
    out = lambda n: pl.BlockSpec((step, n, 8, LANES), lambda i: (i, 0, 0, 0))
    shape = lambda n: jax.ShapeDtypeStruct((levels, n, 8, LANES), F32)
    return pl.pallas_call(
        pack_kernel,
        grid=(levels // step,),
        in_specs=[pl.BlockSpec((NTR, step, ROWS, LANES), lambda i: (0, i, 0, 0)), flow, flow, flow],
        out_specs=[out(3), out(2), out(2), out(2)],
        out_shape=[shape(3), shape(2), shape(2), shape(2)],
        compiler_params=pltpu.CompilerParams(vmem_limit_bytes=VMEM_LIMIT),
        name="pack_halos",
    )(tracers, east, north, mask)


def remap_kernel(n_lon, n_lat, per_step, src, dst, fold, atm, weights, out, blocks, edge, labels, count):
    step = pl.program_id(0)
    devices = n_lon * n_lat

    @pl.when(step == 0)
    def _():
        blocks[...] = jnp.zeros_like(blocks)
        wide = atm[...].astype(F32)
        for b in range(blocks.shape[0]):
            blocks[b, 0:4] = wide[:, b * LANES : (b + 1) * LANES]
        out[...] = jnp.zeros_like(out)
        edge[...] = jnp.zeros_like(edge)
        labels[...] = jnp.zeros_like(labels)

        def clear(i, _):
            count[i] = 0
            return 0

        lax.fori_loop(0, devices, clear, 0)

    lane1 = lanes_of((1, LANES))

    def one(j, _):
        w = step * per_step + j
        place = dst[w]
        lon = place % n_lon
        row = place // n_lon
        local = row % ROWS
        owner = lon * n_lat + row // ROWS
        slot = count[owner]
        count[owner] = slot + 1
        left = blocks[src[w]].astype(jnp.bfloat16)
        product = lax.dot_general(left, weights[j], (((1,), (1,)), ((), ())), preferred_element_type=F32)[0:4]
        out[owner * GROUPS + slot] = product
        labels[pl.ds(owner, 1)] = jnp.where(lane1 == slot, (local + 1).astype(F32), labels[pl.ds(owner, 1)])
        kind = jnp.where(local < 2, local, local - (ROWS - 4))
        is_edge = jnp.logical_or(local < 2, local >= ROWS - 2)
        at = jnp.where(is_edge, owner * 4 + kind, devices * 4)
        edge[at] = edge[at] + product
        return 0

    lax.fori_loop(0, per_step, one, 0, unroll=8)

    @pl.when(step == pl.num_programs(0) - 1)
    def _():
        lane4 = lanes_of((4, LANES))
        high = fold[0] // LANES
        low = fold[0] % LANES
        l_iota = lax.broadcasted_iota(jnp.int32, (LANES, LANES), 0)
        i_iota = lax.broadcasted_iota(jnp.int32, (LANES, LANES), 1)
        reverse = (l_iota == (low - i_iota + LANES) % LANES).astype(F32)
        strips = []
        for p in range(n_lon):
            first = edge[(((high - p + 2 * n_lon) % n_lon) * n_lat + n_lat - 1) * 4 + 3]
            second = edge[(((high - p - 1 + 2 * n_lon) % n_lon) * n_lat + n_lat - 1) * 4 + 3]
            strips.append(jnp.where(lane4 <= low, first, second))
        ghost = jnp.dot(
            jnp.concatenate(strips, 0), reverse, precision=lax.Precision.HIGHEST, preferred_element_type=F32
        )
        packed = []
        for owner in range(devices):
            total = jnp.zeros((4, LANES), F32)
            for n in range(4):
                moved = roll(out[owner * GROUPS + n], 2 + 4 * n)
                total = jnp.where(lane4 // 4 == n, moved, total)
            out[owner * GROUPS + 5] = total
        own = labels[...]
        lane = lanes_of(own.shape)
        west = jnp.concatenate([own[devices - n_lat :], own[: devices - n_lat]], 0)
        east = jnp.concatenate([own[n_lat:], own[:n_lat]], 0)
        both = jnp.where(lane < 4, own, jnp.where(lane < 8, roll(west, 4), roll(east, 8)))
        labels[...] = both
        for lat in range(n_lat):
            packs = [out[(lon * n_lat + lat) * GROUPS + 5] for lon in range(n_lon)]
            for lon in range(n_lon):
                owner = lon * n_lat + lat
                base = owner * GROUPS
                out[base + 4, 0:1] = labels[owner : owner + 1]
                from_west = packs[(lon - 1) % n_lon]
                from_east = packs[(lon + 1) % n_lon]
                out[base + 5] = jnp.where(lane4 < 16, from_west, roll(from_east, 16))
                if lat < n_lat - 1:
                    above = (owner + 1) * 4
                    out[base + 6, 0:2] = edge[above, 0:2]
                    out[base + 6, 2:4] = edge[above + 1, 0:2]
                else:
                    out[base + 6, 0:2] = ghost[4 * lon : 4 * lon + 2]
                    out[base + 6, 2:4] = ghost[4 * lon : 4 * lon + 2]
                if lat > 0:
                    below = (owner - 1) * 4
                    out[base + 7, 0:2] = edge[below + 3, 0:2]
                    out[base + 7, 2:4] = edge[below + 2, 0:2]
                    out[base + 4, 1:2] = edge[below + 3, 3:4]


def remap(atm, weights, src, dst, fold_c, n_lon, n_lat):
    sends = weights.shape[0]
    devices = n_lon * n_lat
    per_step = 32
    blocks = atm.shape[1] // LANES
    return pl.pallas_call(
        functools.partial(remap_kernel, n_lon, n_lat, per_step),
        grid=(sends // per_step,),
        in_specs=[
            pl.BlockSpec(memory_space=pltpu.SMEM),
            pl.BlockSpec(memory_space=pltpu.SMEM),
            pl.BlockSpec(memory_space=pltpu.SMEM),
            pl.BlockSpec(atm.shape, lambda i: (0, 0)),
            pl.BlockSpec((per_step, LANES, LANES), lambda i: (i, 0, 0)),
        ],
        out_specs=pl.BlockSpec((devices * GROUPS, 4, LANES), lambda i: (0, 0, 0)),
        out_shape=jax.ShapeDtypeStruct((devices * GROUPS, 4, LANES), F32),
        scratch_shapes=[
            pltpu.VMEM((blocks, 8, LANES), F32),
            pltpu.VMEM((devices * 4 + 1, 4, LANES), F32),
            pltpu.VMEM((devices, LANES), F32),
            pltpu.SMEM((devices,), jnp.int32),
        ],
        compiler_params=pltpu.CompilerParams(vmem_limit_bytes=VMEM_LIMIT),
        name="remap",
    )(src, dst, fold_c, atm, weights)


def minmod(a, b):
    return jnp.maximum(jnp.minimum(a, b), jnp.minimum(jnp.maximum(a, b), 0.0))


def face_coefficients(flow, mask, drho, zrho):
    diff = DIFFUSIVITY * mask
    strat = 0.25 * zrho
    slope = drho * strat / (strat * strat + SLOPE_EPS)
    up = jnp.maximum(flow, 0.0)
    down = jnp.minimum(flow, 0.0)
    return (
        up + diff,
        down - diff,
        0.5 * up * (1.0 - up),
        -0.5 * down * (1.0 + down),
        0.25 * diff * slope,
    )


def density(temperature, salinity):
    return SALT_BETA_COEFF * salinity - HEAT_ALPHA_COEFF * temperature


def spread(x, lane32):
    for width in (4, 8, 16):
        x = jnp.where(lane32 < width, x, roll(x, width))
    return x


def edge_values(halo, own, lane32):
    hm, h0, hp = halo
    om, o0, op = own
    zh, zo = hp - hm, op - om
    west, first = roll(h0, -1), roll(o0, -2)
    d_west = first - west
    s_west = minmod(d_west, west - h0)
    s_first = minmod(roll(o0, -3) - first, d_west)
    z_west = roll(zh, -1) + roll(zo, -2)
    beyond = roll(h0, -2)
    s_beyond = minmod(roll(h0, -3) - beyond, beyond - roll(o0, -1))
    z_beyond = roll(zh, -2)
    mask = roll(west, -28) * roll(first, -28)
    flow = roll(west, -24) * mask
    coefs = face_coefficients(
        flow, mask, density(d_west, roll(d_west, -4)), density(z_west, roll(z_west, -4))
    )
    a, b, p, q, v = [spread(x, lane32) for x in coefs]
    flux = a * west + b * first + p * s_west + q * s_first + v * z_west
    return beyond, z_beyond, s_beyond, d_west, flux


def level_step(tracer, rows_below, rows_above, halo, own, east, north, land, write, scratch):
    cpad, zpad, spad, fpad, mpad, npad = scratch
    lane8 = lanes_of((8, LANES))
    first_lane = lanes_of((ROWS, LANES)) == 0
    for t in range(NTR):
        cpad[t, 8:72] = tracer(0, t)
        zpad[t, 8:72] = tracer(1, t) - tracer(-1, t)
        for i in range(2):
            cpad[t, 6 + i : 7 + i] = rows_below(0, i, t)
            cpad[t, 72 + i : 73 + i] = rows_above(0, i, t)
        zpad[t, 7:8] = rows_below(1, 1, t) - rows_below(-1, 1, t)
        zpad[t, 72:73] = rows_above(1, 0, t) - rows_above(-1, 0, t)
    mpad[8:72] = land
    mpad[7:8] = rows_below(0, 1, 7)
    mpad[72:73] = rows_above(0, 0, 7)
    npad[8:72] = north
    npad[7:8] = rows_below(0, 1, 6)

    edges = [
        edge_values([halo(j, h) for j in (-1, 0, 1)], [own(j, h) for j in (-1, 0, 1)], lane8 % 32)
        for h in range(2)
    ]

    def at_first(which, f):
        return jnp.concatenate([roll(edges[r // 4][which], -(32 * (r % 4) + 4 * f)) for r in range(8)], 0)

    def eastward(x, which, f):
        return roll(jnp.where(first_lane, at_first(which, f), x), -1)

    def x_parts(t):
        c = cpad[t, 8:72]
        z = zpad[t, 8:72]
        c_east = eastward(c, 0, t)
        return c, c_east, z + eastward(z, 1, t)

    def y_parts(t):
        c = cpad[t, 7:79]
        return c, cpad[t, 8:80], zpad[t, 7:79] + zpad[t, 8:80]

    xs = [x_parts(t) for t in range(2)]
    ys = [y_parts(t) for t in range(2)]
    mask_x = land * eastward(land, 0, 7)
    ax, bx, px, qx, vx = face_coefficients(
        east * mask_x, mask_x, density(xs[0][1] - xs[0][0], xs[1][1] - xs[1][0]), density(xs[0][2], xs[1][2])
    )
    mask_y = mpad[7:79] * mpad[8:80]
    ay, by, py, qy, vy = face_coefficients(
        npad[7:79] * mask_y, mask_y, density(ys[0][1] - ys[0][0], ys[1][1] - ys[1][0]), density(ys[0][2], ys[1][2])
    )
    for t in range(NTR):
        c, c_east, z = xs[t] if t < 2 else x_parts(t)
        d = c_east - c
        s = minmod(d, jnp.where(first_lane, at_first(3, t), roll(d, 1)))
        flux = ax * c + bx * c_east + px * s + qx * eastward(s, 2, t) + vx * z
        result = c - (flux - jnp.where(first_lane, at_first(4, t), roll(flux, 1)))
        c, c_north, z = ys[t] if t < 2 else y_parts(t)
        s = minmod(c_north - c, c - cpad[t, 6:78])
        spad[0:72] = s
        flux = ay * c + by * c_north + py * s + qy * spad[1:73] + vy * z
        fpad[0:72] = flux
        write(t, land * (result - (fpad[1:65] - fpad[0:64])))


def level_scratch():
    return [
        pltpu.VMEM((NTR, 80, LANES), F32),
        pltpu.VMEM((NTR, 80, LANES), F32),
        pltpu.VMEM((80, LANES), F32),
        pltpu.VMEM((80, LANES), F32),
        pltpu.VMEM((80, LANES), F32),
        pltpu.VMEM((80, LANES), F32),
    ]


def deep_kernel(first, below, here, above, east, north, mask, west_cols, east_cols, own_cols, row_below, row_above, out, *scratch):
    k = pl.program_id(0) + first
    levels = own_cols.shape[0]
    level = {-1: k - 1, 0: k, 1: jnp.minimum(k + 1, levels - 1)}
    lane_of_four = lanes_of((8, LANES)) % 4
    sources = {-1: below, 0: here, 1: above}

    def write(t, value):
        out[t, 0] = value

    level_step(
        lambda j, t: sources[j][t, 0],
        lambda j, i, f: row_below[level[j], i, f : f + 1],
        lambda j, i, f: row_above[level[j], i, f : f + 1],
        lambda j, h: jnp.where(lane_of_four < 2, west_cols[level[j], h], east_cols[level[j], h]),
        lambda j, h: own_cols[level[j], h],
        east[0],
        north[0],
        mask[0].astype(F32),
        write,
        scratch,
    )


def deep_levels(first, tracers, east, north, mask, west_cols, east_cols, own_cols, row_below, row_above):
    levels = tracers.shape[1]
    block = (NTR, 1, ROWS, LANES)
    flow = pl.BlockSpec((1, ROWS, LANES), lambda i: (i + first, 0, 0))
    whole = lambda x: pl.BlockSpec(x.shape, lambda i: (0,) * x.ndim)
    return pl.pallas_call(
        functools.partial(deep_kernel, first),
        grid=(levels - first,),
        in_specs=[
            pl.BlockSpec(block, lambda i: (0, i + first - 1, 0, 0)),
            pl.BlockSpec(block, lambda i: (0, i + first, 0, 0)),
            pl.BlockSpec(block, lambda i: (0, jnp.minimum(i + first + 1, levels - 1), 0, 0)),
            flow,
            flow,
            flow,
        ]
        + [whole(x) for x in (west_cols, east_cols, own_cols, row_below, row_above)],
        out_specs=pl.BlockSpec(block, lambda i: (0, i + first, 0, 0)),
        out_shape=jax.ShapeDtypeStruct(tracers.shape, F32),
        scratch_shapes=level_scratch(),
        compiler_params=pltpu.CompilerParams(vmem_limit_bytes=VMEM_LIMIT),
        name="deep_levels",
    )(tracers, tracers, tracers, east, north, mask, west_cols, east_cols, own_cols, row_below, row_above)


def expand(x, lane):
    total = x
    for f in range(2, 6):
        total = jnp.where(lane // 4 == f, roll(x, 4 * (f - 1)), total)
    return jnp.where(lane // 4 == 6, roll(x, 16), total)


def pack_rows(tiles, lane):
    packed = []
    for h in range(2):
        total = jnp.zeros((8, LANES), F32)
        for rr in range(4):
            total = jnp.where(lane // 32 == rr, roll(tiles[4 * h + rr], 32 * rr), total)
        packed.append(total)
    return packed


def force_columns(cols, force, lane):
    field = (lane % 32) // 4
    mask = spread(roll(cols, -28), lane % 32)
    tracer_change = mask * (force * jnp.where(field == 0, HEAT_SCALE, FRESH_SCALE * cols))
    return cols + jnp.where(field < 6, tracer_change, jnp.where(field == 6, STRESS_SCALE * force, 0.0))


def force_rows(rows, mask, heat, fresh, tau):
    field = lax.broadcasted_iota(jnp.int32, (8, LANES), 0)
    tracer_change = mask * jnp.where(field == 0, HEAT_SCALE * heat, FRESH_SCALE * fresh * rows)
    return rows + jnp.where(field < 6, tracer_change, jnp.where(field == 6, STRESS_SCALE * tau, 0.0))


def surface_kernel(
    top, arrived, tracers, east, north, mask, west_cols, east_cols, own_cols, row_below, row_above, _, forcing, out,
    forced, rows_b, rows_a, cols_h, cols_o, *scratch
):
    devices = arrived.shape[0] // (4 * GROUPS)
    stride = 4 * GROUPS
    lane = lanes_of((8, LANES))
    lane_of_four = lane % 4

    def gathered(group, row):
        return arrived[pl.ds(4 * group + row, devices, stride=stride), :]

    labels = gathered(4, 0).T
    row_id = lax.broadcasted_iota(jnp.int32, (ROWS, devices), 0).astype(F32) + 1.0

    def pick(n):
        return (labels[n : n + 1] == row_id).astype(F32)

    def dot(a, b):
        return jnp.dot(a, b, precision=lax.Precision.HIGHEST, preferred_element_type=F32)

    flux = jnp.zeros((ROWS, 4 * LANES), F32)
    for n in range(4):
        flux += dot(pick(n), jnp.concatenate([gathered(n, f) for f in range(4)], 1))
    fields = [flux[:, LANES * f : LANES * (f + 1)] for f in range(4)]
    for f in range(4):
        forcing[f] = fields[f]
    heat, fresh, tau_x, tau_y = fields

    wide = lanes_of((devices, LANES))
    sides = [gathered(5, f) for f in range(3)]
    beside = jnp.zeros((ROWS, LANES), F32)
    for side in range(2):
        for n in range(4):
            back = -4 * n - 16 * side
            lined = jnp.where(
                wide < 4, roll(sides[0], back), jnp.where(wide < 8, roll(sides[1], back + 4), roll(sides[2], back + 8))
            )
            lined = jnp.where((wide < 12) & (wide % 4 // 2 == side), lined, 0.0)
            beside += dot(pick(4 + 4 * side + n), lined)

    def summed(group):
        return jnp.sum(arrived[...].reshape(devices, GROUPS, 4, LANES)[:, group], 0)

    over = [jnp.sum(gathered(6, f), 0, keepdims=True) for f in range(4)]
    under = [jnp.sum(gathered(7, f), 0, keepdims=True) for f in range(4)]
    tau_under = jnp.sum(gathered(4, 1), 0, keepdims=True)

    land = [mask[k].astype(F32) for k in range(2)]
    forced[0] = tracers[0, 0] + land[0] * (HEAT_SCALE * heat)
    for t in range(1, NTR):
        c = tracers[t, 0]
        forced[t] = c + land[0] * (FRESH_SCALE * fresh * c)
    rows_b[0] = force_rows(row_below[0, 0], row_below[0, 0, 7:8], under[2], under[3], 0.0)
    rows_b[1] = force_rows(row_below[0, 1], row_below[0, 1, 7:8], under[0], under[1], tau_under)
    near = jnp.where(top[0] > 0, row_above[0, 1, 7:8], row_above[0, 0, 7:8])
    rows_a[0] = force_rows(row_above[0, 0], near, over[0], over[1], 0.0)
    rows_a[1] = force_rows(row_above[0, 1], row_above[0, 1, 7:8], over[2], over[3], 0.0)
    own_tiles, halo_tiles = [], []
    for r in range(8):
        part = slice(8 * r, 8 * r + 8)
        mine = jnp.where(lane < 4, roll(heat[part], 2), jnp.where(lane < 8, roll(fresh[part], 6), roll(tau_x[part], 10)))
        own_tiles.append(expand(mine, lane))
        halo_tiles.append(expand(beside[part], lane))
    own_force, halo_force = pack_rows(own_tiles, lane), pack_rows(halo_tiles, lane)
    for h in range(2):
        cols = jnp.where(lane_of_four < 2, west_cols[0, h], east_cols[0, h])
        cols_h[h] = force_columns(cols, halo_force[h], lane)
        cols_o[h] = force_columns(own_cols[0, h], own_force[h], lane)

    for k in range(2):

        def at(j):
            return max(k + j, 0)

        def write(t, value):
            out[t, k] = value

        def plain_halo(level, h):
            return jnp.where(lane_of_four < 2, west_cols[level, h], east_cols[level, h])

        level_step(
            lambda j, t: forced[t] if at(j) == 0 else tracers[t, at(j)],
            lambda j, i, f: rows_b[i, f : f + 1] if at(j) == 0 else row_below[at(j), i, f : f + 1],
            lambda j, i, f: rows_a[i, f : f + 1] if at(j) == 0 else row_above[at(j), i, f : f + 1],
            lambda j, h: cols_h[h] if at(j) == 0 else plain_halo(at(j), h),
            lambda j, h: cols_o[h] if at(j) == 0 else own_cols[at(j), h],
            east[k] + STRESS_SCALE * tau_x if k == 0 else east[k],
            north[k] + STRESS_SCALE * tau_y if k == 0 else north[k],
            land[k],
            write,
            scratch,
        )


def surface_levels(top, arrived, tracers, east, north, mask, west_cols, east_cols, own_cols, row_below, row_above, done):
    block = lambda n: pl.BlockSpec((NTR, n, ROWS, LANES), lambda i: (0, 0, 0, 0))
    flow = pl.BlockSpec((2, ROWS, LANES), lambda i: (0, 0, 0))
    halo = lambda x: pl.BlockSpec((3,) + x.shape[1:], lambda i: (0, 0, 0, 0))
    return pl.pallas_call(
        surface_kernel,
        grid=(1,),
        in_specs=[
            pl.BlockSpec(memory_space=pltpu.SMEM),
            pl.BlockSpec(arrived.shape, lambda i: (0, 0)),
            block(3),
            flow,
            flow,
            flow,
        ]
        + [halo(x) for x in (west_cols, east_cols, own_cols, row_below, row_above)]
        + [pl.BlockSpec(memory_space=pl.ANY)],
        out_specs=[pl.BlockSpec((4, ROWS, LANES), lambda i: (0, 0, 0)), block(2)],
        out_shape=[jax.ShapeDtypeStruct((4, ROWS, LANES), F32), jax.ShapeDtypeStruct(tracers.shape, F32)],
        input_output_aliases={11: 1},
        scratch_shapes=[
            pltpu.VMEM((NTR, ROWS, LANES), F32),
            pltpu.VMEM((2, 8, LANES), F32),
            pltpu.VMEM((2, 8, LANES), F32),
            pltpu.VMEM((2, 8, LANES), F32),
            pltpu.VMEM((2, 8, LANES), F32),
        ]
        + level_scratch(),
        compiler_params=pltpu.CompilerParams(vmem_limit_bytes=VMEM_LIMIT),
        name="surface_levels",
    )(top, arrived, tracers, east, north, mask, west_cols, east_cols, own_cols, row_below, row_above, done)


def fold_ghost(own_top, west_top, c, n_lon, n_lat):
    low = c % LANES
    lane = jnp.arange(LANES)
    joined = jnp.where(lane <= low, own_top, west_top)
    reverse = (lane[:, None] == (low - lane[None, :]) % LANES).astype(F32)
    strip = jnp.einsum("kfl,li->kfi", joined, reverse, precision=lax.Precision.HIGHEST, preferred_element_type=F32)

    def move(b):
        pairs = [(q * n_lat + n_lat - 1, ((b - q) % n_lon) * n_lat + n_lat - 1) for q in range(n_lon)]
        return lambda x: lax.ppermute(x, ("lon", "lat"), pairs)

    return lax.switch(c // LANES, [move(b) for b in range(n_lon)], strip)


def body(tracers, flow_east, flow_north, sea_mask, atm_fields, remap_weights, remap_src, remap_dst, fold_partner):
    n_lon, n_lat = lax.axis_size("lon"), lax.axis_size("lat")
    devices = n_lon * n_lat
    lon, lat = lax.axis_index("lon"), lax.axis_index("lat")
    columns = n_lon * LANES
    c = (fold_partner[0] + lon * LANES) % columns

    outgoing = remap(atm_fields, remap_weights, remap_src, remap_dst, c[None], n_lon, n_lat)
    arrived = lax.all_to_all(
        outgoing.reshape(devices, 4 * GROUPS, LANES), ("lon", "lat"), split_axis=0, concat_axis=0, tiled=True
    )

    both, own_cols, up, down = pack_halos(tracers, flow_east, flow_north, sea_mask)
    right = [(i, (i + 1) % n_lon) for i in range(n_lon)]
    left = [(j, i) for i, j in right]
    north = [(i, i + 1) for i in range(n_lat - 1)]
    south = [(j, i) for i, j in north]
    west_cols = lax.ppermute(both, "lon", right)
    east_cols = lax.ppermute(own_cols, "lon", left)
    row_below = lax.ppermute(up, "lat", north)
    row_above = lax.ppermute(down, "lat", south)
    ghost = fold_ghost(both[:, 2], west_cols[:, 2], c, n_lon, n_lat)
    is_top = lat == n_lat - 1
    field = jnp.arange(8)[:, None]
    ghost_rows = jnp.stack([jnp.where(field == 7, 1.0, ghost), ghost], 1)
    row_above = jnp.where(is_top, ghost_rows, row_above)
    halos = (west_cols, east_cols, own_cols, row_below, row_above)

    done = deep_levels(2, tracers, flow_east, flow_north, sea_mask, *halos)
    top = is_top.astype(jnp.int32)[None]
    return surface_levels(
        top, arrived.reshape(devices * 4 * GROUPS, LANES), tracers, flow_east, flow_north, sea_mask, *halos, done
    )


def solution(mesh):
    placed = (
        P(None, None, "lat", "lon"),
        P(None, "lat", "lon"),
        P(None, "lat", "lon"),
        P(None, "lat", "lon"),
        P(None, ("lon", "lat")),
        P(("lon", "lat"), None, None),
        P(("lon", "lat")),
        P(("lon", "lat")),
        P("lon"),
    )
    return jax.shard_map(
        body,
        mesh=mesh,
        in_specs=placed,
        out_specs=(P(None, "lat", "lon"), P(None, None, "lat", "lon")),
        check_vma=False,
    )
```

profile of v0, /device:TPU:2, one launch (start us, length us, event | category | flops | bytes accessed | tf_op | source)
XLA Modules:
  0.0 109.3 jit_solution(9003332847388642519)
XLA Ops:
  1.3 13.8 %remap.1 = f32[1024,4,128]{2,1,0:T(4,128)} custom-call(s32[256]{0:T(256)} %src.1, s32[256]{0:T(256)} %dst.1, s32[1]{0:T(128)} %bitcast.2.fold, bf16[4,8192]{1,0:T(4,128)(2,1)} %atm.1, bf16[256,128,128]{2,1,0:T(8,128)(2,1)} %weights.1), custom_call_target="tpu_custom_call" | custom-call | tf_op jit(solution)/shard_map/remap/pallas_call | solution.py:174
  15.1 10.5 %all-to-all-start = ((f32[128,32,128]{2,1,0:T(8,128)}), f32[128,32,128]{2,1,0:T(8,128)S(1)}, u32[]{:S(2)}, u32[]{:S(2)}) async-start(f32[128,32,128]{2,1,0:T(8,128)} %bitcast.23), calls=%async_computation | async-start | bytes 4194304 | tf_op jit(solution)/shard_map/all_to_all | solution.py:551
  25.6 8.9 %pack_halos.1 = (f32[24,3,8,128]{3,2,1,0:T(8,128)}, f32[24,2,8,128]{3,2,1,0:T(8,128)}, f32[24,2,8,128]{3,2,1,0:T(8,128)}, f32[24,2,8,128]{3,2,1,0:T(8,128)}) custom-call(f32[6,24,64,128]{3,2,1,0:T(8,128)} %tracers.3, f32[24,64,128]{2,1,0:T(8,128)} %east.5, f32[24,64,128]{2,1,0:T(8,128)} %north.5, s32[24,64,128]{2,1,0:T(8,128)} %mask.5), custom_call_target="tpu_custom_call" | custom-call | tf_op jit(solution)/shard_map/pack_halos/pallas_call | solution.py:63
  34.5 3.5 %collective-permute-start.18 = (f32[24,2,8,128]{3,2,1,0:T(8,128)}, f32[24,2,8,128]{3,2,1,0:T(8,128)S(1)}, u32[]{:S(2)}, u32[]{:S(2)}) collective-permute-start(f32[24,2,8,128]{3,2,1,0:T(8,128)} %get-tuple-element.41), channel_id=1, source_target_pairs={{0,1},{1,2},{2,3},{3,4},{4,5},{5,6},{6,7},{8,9},{9,10},{10,11},{11... | collective-permute-start | bytes 589832 | tf_op jit(solution)/shard_map/ppermute | solution.py:562
  38.0 4.4 %collective-permute-start.19 = (f32[24,2,8,128]{3,2,1,0:T(8,128)}, f32[24,2,8,128]{3,2,1,0:T(8,128)S(1)}, u32[]{:S(2)}, u32[]{:S(2)}) collective-permute-start(f32[24,2,8,128]{3,2,1,0:T(8,128)} %get-tuple-element.42), channel_id=1, source_target_pairs={{1,0},{2,1},{3,2},{4,3},{5,4},{6,5},{7,6},{9,8},{10,9},{11,10},{12... | collective-permute-start | bytes 589832 | tf_op jit(solution)/shard_map/ppermute | solution.py:563
  42.4 3.5 %collective-permute-start.17 = (f32[24,2,8,128]{3,2,1,0:T(8,128)}, f32[24,2,8,128]{3,2,1,0:T(8,128)S(1)}, u32[]{:S(2)}, u32[]{:S(2)}) collective-permute-start(f32[24,2,8,128]{3,2,1,0:T(8,128)} %get-tuple-element.40.own_cols), channel_id=1, source_target_pairs={{8,0},{16,8},{24,16},{32,24},{40,32},{48,40},{56,48},{64,56},{72,6... | collective-permute-start | bytes 589832 | tf_op jit(solution)/shard_map/ppermute | solution.py:561
  46.0 0.0 collective-permute-start.16
  46.0 17.1 %collective-permute-done.16.west_cols = f32[24,3,8,128]{3,2,1,0:T(8,128)S(1)} collective-permute-done((f32[24,3,8,128]{3,2,1,0:T(8,128)}, f32[24,3,8,128]{3,2,1,0:T(8,128)S(1)}, u32[]{:S(2)}, u32[]{:S(2)}) %collective-permute-start.16) | collective-permute-done | bytes 294944 | tf_op jit(solution)/shard_map/ppermute | solution.py:560
  63.1 1.2 %fusion.1 = f32[24,8,128]{2,1,0:T(8,128)S(1)} fusion(f32[24,3,8,128]{3,2,1,0:T(8,128)S(1)} %collective-permute-done.16.west_cols, pred[128]{0:T(512)(128)(4,1)S(1)} %iota_compare_fusion.1, s32[128]{0:T(128)S(1)} %and_select_fusion, f32[24,3,8,128]{3,2,1,0:T(8,128)} %get-tuple-element.39), kind=kOutput, calls=%fused_computation.3 | convolution fusion | flops 37789696 | bytes 295936 | tf_op jit(solution)/shard_map/kfl,li->kfi/dot_general | solution.py:534
  64.3 1.3 %conditional.1 = (f32[24,8,128]{2,1,0:T(8,128)}) conditional(s32[]{:T(128)} %clamp.3, f32[24,8,128]{2,1,0:T(8,128)S(1)} %fusion.1, f32[24,8,128]{2,1,0:T(8,128)S(1)} %fusion.1, f32[24,8,128]{2,1,0:T(8,128)S(1)} %fusion.1, f32[24,8,128]{2,1,0:T(8,128)S(1)} %fusion.1, f32[24,8,128]{2,1,0:T(8,128)S(1)} %fusion.1, ...), branch_computations={%region_0.1_spmd, %region_1.2_spmd, %region_2.3_spmd, %region_3.4_... | conditional | bytes 393264 | solution.py:540
  64.3 1.3 %collective-permute-start.13 = (f32[24,8,128]{2,1,0:T(8,128)S(1)}, f32[24,8,128]{2,1,0:T(8,128)}, u32[]{:S(2)}, u32[]{:S(2)}) collective-permute-start(f32[24,8,128]{2,1,0:T(8,128)S(1)} %param.13), channel_id=1, source_target_pairs={{7,111},{15,103},{23,95},{31,87},{39,79},{47,71},{55,63},{63,55},{... | collective-permute-start | bytes 294920 | tf_op jit(solution)/shard_map/cond/branch_13_fun/ppermute | solution.py:538
  65.6 0.0 collective-permute-done.13
  65.6 1.0 select_bitcast_fusion
  66.6 0.0 collective-permute-done.19
  66.6 1.6 %maximum_select_fusion.row_above = f32[24,2,8,128]{3,2,1,0:T(8,128)} fusion(f32[24,2,8,128]{3,2,1,0:T(8,128)S(1)} %collective-permute-done.19, f32[24,1,8,128]{3,2,1,0:T(8,128)} %bitcast.9, f32[24,1,8,128]{3,2,1,0:T(8,128)S(1)} %select_bitcast_fusion, pred[]{:T(512)S(6)} %eq.27), kind=kLoop, calls=%fused_computation | loop fusion | flops 98304 | bytes 589825 | tf_op jit(solution)/shard_map/jit(_where)/select_n | solution.py:568
  68.2 0.0 collective-permute-done.18.row_below
  68.2 0.0 collective-permute-done.17.east_cols
  68.2 0.0 copy-done.1
  68.2 0.7 copy-done.2
  68.9 0.7 copy-done.3
  69.6 31.2 %deep_levels.1._ = f32[6,24,64,128]{3,2,1,0:T(8,128)} custom-call(f32[6,24,64,128]{3,2,1,0:T(8,128)} %tracers.3, f32[6,24,64,128]{3,2,1,0:T(8,128)} %tracers.3, f32[6,24,64,128]{3,2,1,0:T(8,128)} %tracers.3, f32[24,64,128]{2,1,0:T(8,128)} %east.5, f32[24,64,128]{2,1,0:T(8,128)} %north.5, s32[24,64,128]{2,1,0:T(8,128)} %mask.5, f32[24,3,8,128]{3,2,1,0:T(8,128)} %copy-done.1, ...), custom_call_target="tpu_custom_call" | custom-call | tf_op jit(solution)/shard_map/deep_levels/pallas_call | solution.py:351
  100.8 0.0 all-to-all-done
  100.8 1.3 %copy-done = f32[128,32,128]{2,1,0:T(8,128)} copy-done((f32[128,32,128]{2,1,0:T(8,128)}, f32[128,32,128]{2,1,0:T(8,128)S(1)}, u32[]{:S(2)}) %copy-start) | copy-done | bytes 2097176
  102.1 7.2 %surface_levels.1 = (f32[4,64,128]{2,1,0:T(8,128)}, f32[6,24,64,128]{3,2,1,0:T(8,128)}) custom-call(s32[1]{0:T(128)} %bitcast.top, f32[4096,128]{1,0:T(8,128)} %bitcast.22, f32[6,24,64,128]{3,2,1,0:T(8,128)} %tracers.3, f32[24,64,128]{2,1,0:T(8,128)} %east.5, f32[24,64,128]{2,1,0:T(8,128)} %north.5, ...), custom_call_target="tpu_custom_call", output_to_operand_aliasing={{1}: (11, {})} | custom-call | tf_op jit(solution)/shard_map/surface_levels/pallas_call | solution.py:500
  (7 shorter events, 0.0 us)
Async XLA Ops:
  15.1 85.7 %all-to-all-start = ((f32[128,32,128]{2,1,0:T(8,128)}), f32[128,32,128]{2,1,0:T(8,128)S(1)}, u32[]{:S(2)}, u32[]{:S(2)}) async-start(f32[128,32,128]{2,1,0:T(8,128)} %bitcast.23), calls=%async_computation | async-start | bytes 4194304 | tf_op jit(solution)/shard_map/all_to_all | solution.py:551
  34.5 33.7 %collective-permute-start.18 = (f32[24,2,8,128]{3,2,1,0:T(8,128)}, f32[24,2,8,128]{3,2,1,0:T(8,128)S(1)}, u32[]{:S(2)}, u32[]{:S(2)}) collective-permute-start(f32[24,2,8,128]{3,2,1,0:T(8,128)} %get-tuple-element.41), channel_id=1, source_target_pairs={{0,1},{1,2},{2,3},{3,4},{4,5},{5,6},{6,7},{8,9},{9,10},{10,11},{11... | collective-permute-start | bytes 589832 | tf_op jit(solution)/shard_map/ppermute | solution.py:562
  38.0 28.6 %collective-permute-start.19 = (f32[24,2,8,128]{3,2,1,0:T(8,128)}, f32[24,2,8,128]{3,2,1,0:T(8,128)S(1)}, u32[]{:S(2)}, u32[]{:S(2)}) collective-permute-start(f32[24,2,8,128]{3,2,1,0:T(8,128)} %get-tuple-element.42), channel_id=1, source_target_pairs={{1,0},{2,1},{3,2},{4,3},{5,4},{6,5},{7,6},{9,8},{10,9},{11,10},{12... | collective-permute-start | bytes 589832 | tf_op jit(solution)/shard_map/ppermute | solution.py:563
  42.4 25.8 %collective-permute-start.17 = (f32[24,2,8,128]{3,2,1,0:T(8,128)}, f32[24,2,8,128]{3,2,1,0:T(8,128)S(1)}, u32[]{:S(2)}, u32[]{:S(2)}) collective-permute-start(f32[24,2,8,128]{3,2,1,0:T(8,128)} %get-tuple-element.40.own_cols), channel_id=1, source_target_pairs={{8,0},{16,8},{24,16},{32,24},{40,32},{48,40},{56,48},{64,56},{72,6... | collective-permute-start | bytes 589832 | tf_op jit(solution)/shard_map/ppermute | solution.py:561
  46.0 17.1 %collective-permute-start.16 = (f32[24,3,8,128]{3,2,1,0:T(8,128)}, f32[24,3,8,128]{3,2,1,0:T(8,128)S(1)}, u32[]{:S(2)}, u32[]{:S(2)}) collective-permute-start(f32[24,3,8,128]{3,2,1,0:T(8,128)} %get-tuple-element.39), channel_id=1, source_target_pairs={{0,8},{8,16},{16,24},{24,32},{32,40},{40,48},{48,56},{56,64},{64,7... | collective-permute-start | bytes 884744 | tf_op jit(solution)/shard_map/ppermute | solution.py:560
  63.1 5.1 %copy-start.1 = (f32[24,3,8,128]{3,2,1,0:T(8,128)}, f32[24,3,8,128]{3,2,1,0:T(8,128)S(1)}, u32[]{:S(2)}) copy-start(f32[24,3,8,128]{3,2,1,0:T(8,128)S(1)} %collective-permute-done.16.west_cols) | copy-start | bytes 884740
  64.3 1.3 %collective-permute-start.13 = (f32[24,8,128]{2,1,0:T(8,128)S(1)}, f32[24,8,128]{2,1,0:T(8,128)}, u32[]{:S(2)}, u32[]{:S(2)}) collective-permute-start(f32[24,8,128]{2,1,0:T(8,128)S(1)} %param.13), channel_id=1, source_target_pairs={{7,111},{15,103},{23,95},{31,87},{39,79},{47,71},{55,63},{63,55},{... | collective-permute-start | bytes 294920 | tf_op jit(solution)/shard_map/cond/branch_13_fun/ppermute | solution.py:538
  68.2 0.7 copy-start.2
  68.9 0.7 copy-start.3
  100.8 1.3 %copy-start = (f32[128,32,128]{2,1,0:T(8,128)}, f32[128,32,128]{2,1,0:T(8,128)S(1)}, u32[]{:S(2)}) copy-start(f32[128,32,128]{2,1,0:T(8,128)S(1)} %all-to-all-done) | copy-start | bytes 6291460
where the time goes:
time: 110 us; the launch traced here: 109 us
  Pallas kernels  61.1 us (56%)
  starting transfers between devices  23.3 us (21%)
  waiting for transfers between devices  17.1 us (16%)
  local copies, waits for them, and re-layouts  2.67 us (2%)
  other arithmetic  2.58 us (2%)
  between operations  1.37 us (1%)
  matrix products  1.18 us (1%)
    pallas_call x1, Pallas kernels, deep_levels(): pl.pallas_call(functools.partial(deep_kernel, first), grid=(levels - firs...  31.2 us
    ppermute x1, waiting for transfers between devices, body(): west_cols = lax.ppermute(both, 'lon', right)  17.1 us
    pallas_call x1, Pallas kernels, remap(): pl.pallas_call(functools.partial(remap_kernel, n_lon, n_lat, per_step), g...  13.8 us
    all_to_all x1, starting transfers between devices, body(): lax.all_to_all(outgoing.reshape(devices, 4 * GROUPS, LANES), ('lon', 'lat...  10.5 us
    pallas_call x1, Pallas kernels, pack_halos(): pl.pallas_call(pack_kernel, grid=(levels // step,), in_specs=[pl.BlockSpe...  8.87 us
    pallas_call x1, Pallas kernels, surface_levels(): pl.pallas_call(surface_kernel, grid=(1,), in_specs=[pl.BlockSpec(memory_s...  7.19 us
    ppermute x1, starting transfers between devices, body(): row_above = lax.ppermute(down, 'lat', south)  4.44 us
    ppermute x1, starting transfers between devices, body(): east_cols = lax.ppermute(own_cols, 'lon', left)  3.54 us
  transfers between devices with their start and end apart: 6, of which 1 were waited for; matrix products, arithmetic and copies ran while one was open for 3% of the time, Pallas kernels for 37%

commit v1 on v0

--- a/solution.py
+++ b/solution.py
@@ -20,6 +20,8 @@
 LANES = 128
 GROUPS = 8
 F32 = jnp.float32
+TOGETHER = 2
+EDGE_LEVELS = 8
 VMEM_LIMIT = 56 * 1024 * 1024
 
 
@@ -34,29 +36,40 @@
 def pack_kernel(tracers, east, north, mask, both_ref, cols_ref, up_ref, down_ref):
     lane_group = lanes_of((8, LANES)) // 4
     levels = east.shape[0]
-    for k in range(levels):
+    def one(k, _):
         land = mask[k].astype(F32)
-        fields = [tracers[t, k] for t in range(NTR)] + [east[k], land]
         for h in range(2):
             total = jnp.zeros((8, LANES), F32)
             for rr in range(4):
                 start = (4 * h + rr) * 8
                 for f in range(8):
-                    moved = roll(fields[f][start : start + 8], 2 + 32 * rr + 4 * f)
+                    if f < NTR:
+                        tile = tracers[f, k, start : start + 8]
+                    else:
+                        tile = land[start : start + 8] if f == 7 else east[k, start : start + 8]
+                    moved = roll(tile, 2 + 32 * rr + 4 * f)
                     total = jnp.where(lane_group == 8 * rr + f, moved, total)
             both_ref[k, h] = total
             cols_ref[k, h] = total
-        fields[6] = north[k]
+
+        def row(f, r):
+            if f < NTR:
+                return tracers[f, k, r : r + 1]
+            return land[r : r + 1] if f == 7 else north[k, r : r + 1]
+
         for f in range(8):
-            both_ref[k, 2, f : f + 1] = fields[f][ROWS - 1 : ROWS]
+            both_ref[k, 2, f : f + 1] = row(f, ROWS - 1)
             for i in range(2):
-                up_ref[k, i, f : f + 1] = fields[f][ROWS - 2 + i : ROWS - 1 + i]
-                down_ref[k, i, f : f + 1] = fields[f][i : i + 1]
+                up_ref[k, i, f : f + 1] = row(f, ROWS - 2 + i)
+                down_ref[k, i, f : f + 1] = row(f, i)
+        return 0
+
+    lax.fori_loop(0, levels, one, 0)
 
 
 def pack_halos(tracers, east, north, mask):
     levels = east.shape[0]
-    step = 2
+    step = 6
     flow = pl.BlockSpec((step, ROWS, LANES), lambda i: (i, 0, 0))
     out = lambda n: pl.BlockSpec((step, n, 8, LANES), lambda i: (i, 0, 0, 0))
     shape = lambda n: jax.ShapeDtypeStruct((levels, n, 8, LANES), F32)
@@ -92,27 +105,34 @@
         lax.fori_loop(0, devices, clear, 0)
 
     lane1 = lanes_of((1, LANES))
-
-    def one(j, _):
-        w = step * per_step + j
-        place = dst[w]
-        lon = place % n_lon
-        row = place // n_lon
-        local = row % ROWS
-        owner = lon * n_lat + row // ROWS
-        slot = count[owner]
-        count[owner] = slot + 1
-        left = blocks[src[w]].astype(jnp.bfloat16)
-        product = lax.dot_general(left, weights[j], (((1,), (1,)), ((), ())), preferred_element_type=F32)[0:4]
-        out[owner * GROUPS + slot] = product
-        labels[pl.ds(owner, 1)] = jnp.where(lane1 == slot, (local + 1).astype(F32), labels[pl.ds(owner, 1)])
-        kind = jnp.where(local < 2, local, local - (ROWS - 4))
-        is_edge = jnp.logical_or(local < 2, local >= ROWS - 2)
-        at = jnp.where(is_edge, owner * 4 + kind, devices * 4)
-        edge[at] = edge[at] + product
+    batch = 8
+
+    def several(i, _):
+        places, lefts = [], []
+        for j in range(batch):
+            w = step * per_step + batch * i + j
+            place = dst[w]
+            lon = place & (n_lon - 1) if n_lon & (n_lon - 1) == 0 else place % n_lon
+            row = place // n_lon
+            local = row % ROWS
+            owner = lon * n_lat + row // ROWS
+            slot = count[owner]
+            count[owner] = slot + 1
+            kind = jnp.where(local < 2, local, local - (ROWS - 4))
+            is_edge = jnp.logical_or(local < 2, local >= ROWS - 2)
+            places.append((owner, slot, local, jnp.where(is_edge, owner * 4 + kind, devices * 4)))
+            lefts.append(blocks[src[w], 0:4])
+        left = jnp.concatenate(lefts, 0).astype(jnp.bfloat16)
+        right = weights[pl.ds(pl.multiple_of(batch * i, batch), batch)].reshape(batch * LANES, LANES)
+        products = lax.dot_general(left, right, (((1,), (1,)), ((), ())), preferred_element_type=F32)
+        for j, (owner, slot, local, at) in enumerate(places):
+            product = products[4 * j : 4 * j + 4, LANES * j : LANES * (j + 1)]
+            out[owner * GROUPS + slot] = product
+            labels[pl.ds(owner, 1)] = jnp.where(lane1 == slot, (local + 1).astype(F32), labels[pl.ds(owner, 1)])
+            edge[at] = edge[at] + product
         return 0
 
-    lax.fori_loop(0, per_step, one, 0, unroll=8)
+    lax.fori_loop(0, per_step // batch, several, 0, unroll=2)
 
     @pl.when(step == pl.num_programs(0) - 1)
     def _():
@@ -223,149 +243,289 @@
     return x
 
 
-def edge_values(halo, own, lane32):
-    hm, h0, hp = halo
-    om, o0, op = own
-    zh, zo = hp - hm, op - om
-    west, first = roll(h0, -1), roll(o0, -2)
-    d_west = first - west
-    s_west = minmod(d_west, west - h0)
-    s_first = minmod(roll(o0, -3) - first, d_west)
-    z_west = roll(zh, -1) + roll(zo, -2)
-    beyond = roll(h0, -2)
-    s_beyond = minmod(roll(h0, -3) - beyond, beyond - roll(o0, -1))
-    z_beyond = roll(zh, -2)
-    mask = roll(west, -28) * roll(first, -28)
-    flow = roll(west, -24) * mask
-    coefs = face_coefficients(
-        flow, mask, density(d_west, roll(d_west, -4)), density(z_west, roll(z_west, -4))
+def edge_values(halo, own):
+    lane = lanes_of(halo(0, 0).shape)
+    lane4, lane32 = lane % 4, lane % 32
+    east = lane4 == 0
+    parts = []
+    for h in range(2):
+        p, o = halo(0, h), own(0, h)
+        zp, zo = halo(1, h) - halo(-1, h), own(1, h) - own(-1, h)
+        o1, p2, zp2 = roll(o, -1), roll(p, -2), roll(zp, -2)
+        zo1 = roll(zo, -1)
+        parts.append(
+            (
+                jnp.where(east, o, roll(p, 1)),
+                jnp.where(east, o1, p),
+                jnp.where(east, p2, o1),
+                jnp.where(east, roll(p, -3), roll(o, -2)),
+                jnp.where(east, zo1, zp),
+                jnp.where(east, zp2, zo1),
+            )
+        )
+    c0, c1, c2, c3, z1, z2 = [jnp.where(lane4 < 2, x, roll(y, 2)) for x, y in zip(*parts)]
+    d2 = c2 - c1
+    s1, s2 = minmod(d2, c1 - c0), minmod(c3 - c2, d2)
+    z = z1 + z2
+    mask = roll(c1 * c2, -28)
+    coefs = face_coefficients(roll(c1, -24) * mask, mask, density(d2, roll(d2, -4)), density(z, roll(z, -4)))
+    a, b, p, q, v = [spread(x, lane32) for x in coefs]
+    return jnp.where(lane4 % 2 == 0, s1, s2), a * c1 + b * c2 + p * s1 + q * s2 + v * z
+
+
+def in_step(*levels):
+    levels = list(levels)
+    while levels:
+        levels = [level for level in levels if next(level, None) is not None]
+
+
+def level_step(below, cpad, above, rows_below, rows_above, edge_slope, edge_flux, east, north, land, write, scratch):
+    zpad, hpad, gpad, slope, xco, yco, mpad, tops = scratch
+    lane = lanes_of((8, LANES))
+    first_lane, last_lane = lane == 0, lane == LANES - 1
+    mid = slice(8, 72)
+
+    below1, below2 = rows_below(0, 1), rows_below(0, 0)
+    above1, above2 = rows_above(0, 0), rows_above(0, 1)
+    z_below = rows_below(1, 1) - rows_below(-1, 1)
+    z_above = rows_above(1, 0) - rows_above(-1, 0)
+    for t in range(NTR):
+        zpad[t, mid] = above[t, mid] - below[t, mid]
+        cpad[t, 7:8] = below1[t : t + 1]
+        cpad[t, 72:73] = above1[t : t + 1]
+        tops[0, t : t + 1] = cpad[t, 8:9]
+        tops[1, t : t + 1] = cpad[t, 71:72]
+    for t in range(2):
+        zpad[t, 72:73] = z_above[t : t + 1]
+    tops[2] = zpad[0, 8:16]
+    tops[3] = zpad[1, 8:16]
+    mpad[mid] = land
+    mpad[72:73] = above1[7:8]
+
+    yield True
+
+    def at_edge(x, r, f):
+        return roll(x, -(32 * (r % 4) + 4 * f + 2 * (r // 4) + 1))
+
+    def x_face(t):
+        c, z = cpad[t, mid], zpad[t, mid]
+        return roll(c, -1) - c, z + roll(z, -1)
+
+    (dt, zt), (ds, zs) = x_face(0), x_face(1)
+    mask = land * roll(land, -1)
+    a, b, p, q, v = face_coefficients(east * mask, mask, density(dt, ds), density(zt, zs))
+    for i, x in enumerate((a, p, v, roll(b, 1), roll(q, 1), roll(v, 1))):
+        xco[i] = x
+    yield True
+
+    def y_face(t):
+        return cpad[t, 9:73] - cpad[t, mid], zpad[t, mid] + zpad[t, 9:73]
+
+    (dt, zt), (ds, zs) = y_face(0), y_face(1)
+    mask = land * mpad[9:73]
+    for i, x in enumerate(face_coefficients(north * mask, mask, density(dt, ds), density(zt, zs))):
+        yco[i, mid] = x
+    row0 = tops[0]
+    mask = below1[7:8] * mpad[8:9]
+    d = row0 - below1
+    a, b, p, q, v = face_coefficients(
+        below1[6:7] * mask,
+        mask,
+        density(d[0:1], d[1:2]),
+        density(z_below[0:1] + tops[2, 0:1], z_below[1:2] + tops[3, 0:1]),
     )
-    a, b, p, q, v = [spread(x, lane32) for x in coefs]
-    flux = a * west + b * first + p * s_west + q * s_first + v * z_west
-    return beyond, z_beyond, s_beyond, d_west, flux
-
-
-def level_step(tracer, rows_below, rows_above, halo, own, east, north, land, write, scratch):
-    cpad, zpad, spad, fpad, mpad, npad = scratch
-    lane8 = lanes_of((8, LANES))
-    first_lane = lanes_of((ROWS, LANES)) == 0
+    yco[1, 7:8], yco[3, 7:8], yco[4, 7:8] = b, q, v
+    h_below = a * below1 + p * minmod(d, below1 - below2) + v * z_below
+    b, q, v = yco[1, 71:72], yco[3, 71:72], yco[4, 71:72]
+    g_above = b * above1 + q * minmod(above2 - above1, above1 - tops[1]) + v * z_above
     for t in range(NTR):
-        cpad[t, 8:72] = tracer(0, t)
-        zpad[t, 8:72] = tracer(1, t) - tracer(-1, t)
-        for i in range(2):
-            cpad[t, 6 + i : 7 + i] = rows_below(0, i, t)
-            cpad[t, 72 + i : 73 + i] = rows_above(0, i, t)
-        zpad[t, 7:8] = rows_below(1, 1, t) - rows_below(-1, 1, t)
-        zpad[t, 72:73] = rows_above(1, 0, t) - rows_above(-1, 0, t)
-    mpad[8:72] = land
-    mpad[7:8] = rows_below(0, 1, 7)
-    mpad[72:73] = rows_above(0, 0, 7)
-    npad[8:72] = north
-    npad[7:8] = rows_below(0, 1, 6)
-
-    edges = [
-        edge_values([halo(j, h) for j in (-1, 0, 1)], [own(j, h) for j in (-1, 0, 1)], lane8 % 32)
-        for h in range(2)
+        hpad[t, 7:8] = h_below[t : t + 1]
+        gpad[t, 72:73] = g_above[t : t + 1]
+
+    yield True
+    at_side = jnp.logical_or(first_lane, last_lane)
+    for r in range(8):
+        here = slice(8 + 8 * r, 16 + 8 * r)
+        lower, upper = slice(7 + 8 * r, 15 + 8 * r), slice(9 + 8 * r, 17 + 8 * r)
+        ya, yp, yv, yb, yq, yw = yco[0, here], yco[2, here], yco[4, here], yco[1, lower], yco[3, lower], yco[4, lower]
+        for t in range(NTR):
+            c, z = cpad[t, here], zpad[t, here]
+            s = minmod(roll(c, -1) - c, c - roll(c, 1))
+            slope[t, 8 * r : 8 * r + 8] = jnp.where(at_side, at_edge(edge_slope, r, t), s)
+            s = minmod(cpad[t, upper] - c, c - cpad[t, lower])
+            hpad[t, here] = ya * c + yp * s + yv * z
+            gpad[t, here] = yb * c + yq * s + yw * z
+        yield True
+    for r in range(8):
+        here = slice(8 + 8 * r, 16 + 8 * r)
+        lower, upper = slice(7 + 8 * r, 15 + 8 * r), slice(9 + 8 * r, 17 + 8 * r)
+        part = slice(8 * r, 8 * r + 8)
+        xa, xp, xv, xb, xq, xw = [xco[i, part] for i in range(6)]
+        wet = mpad[here]
+        for t in range(NTR):
+            c, z, s = cpad[t, here], zpad[t, here], slope[t, part]
+            h = xa * c + xp * s + xv * z
+            g = xb * c + xq * s + xw * z
+            flux = at_edge(edge_flux, r, t)
+            out_east = jnp.where(last_lane, flux, h + roll(g, -1))
+            in_west = jnp.where(first_lane, flux, g + roll(h, 1))
+            out_north = hpad[t, here] + gpad[t, upper]
+            in_south = hpad[t, lower] + gpad[t, here]
+            write(t, part, wet * (c - (out_east - in_west) - (out_north - in_south)))
+        yield True
+
+
+def level_scratch():
+    padded = pltpu.VMEM((NTR, 80, LANES), F32)
+    return [
+        padded,
+        padded,
+        padded,
+        pltpu.VMEM((NTR, ROWS, LANES), F32),
+        pltpu.VMEM((6, ROWS, LANES), F32),
+        pltpu.VMEM((5, 80, LANES), F32),
+        pltpu.VMEM((80, LANES), F32),
+        pltpu.VMEM((4, 8, LANES), F32),
     ]
 
-    def at_first(which, f):
-        return jnp.concatenate([roll(edges[r // 4][which], -(32 * (r % 4) + 4 * f)) for r in range(8)], 0)
-
-    def eastward(x, which, f):
-        return roll(jnp.where(first_lane, at_first(which, f), x), -1)
-
-    def x_parts(t):
-        c = cpad[t, 8:72]
-        z = zpad[t, 8:72]
-        c_east = eastward(c, 0, t)
-        return c, c_east, z + eastward(z, 1, t)
-
-    def y_parts(t):
-        c = cpad[t, 7:79]
-        return c, cpad[t, 8:80], zpad[t, 7:79] + zpad[t, 8:80]
-
-    xs = [x_parts(t) for t in range(2)]
-    ys = [y_parts(t) for t in range(2)]
-    mask_x = land * eastward(land, 0, 7)
-    ax, bx, px, qx, vx = face_coefficients(
-        east * mask_x, mask_x, density(xs[0][1] - xs[0][0], xs[1][1] - xs[1][0]), density(xs[0][2], xs[1][2])
-    )
-    mask_y = mpad[7:79] * mpad[8:80]
-    ay, by, py, qy, vy = face_coefficients(
-        npad[7:79] * mask_y, mask_y, density(ys[0][1] - ys[0][0], ys[1][1] - ys[1][0]), density(ys[0][2], ys[1][2])
-    )
-    for t in range(NTR):
-        c, c_east, z = xs[t] if t < 2 else x_parts(t)
-        d = c_east - c
-        s = minmod(d, jnp.where(first_lane, at_first(3, t), roll(d, 1)))
-        flux = ax * c + bx * c_east + px * s + qx * eastward(s, 2, t) + vx * z
-        result = c - (flux - jnp.where(first_lane, at_first(4, t), roll(flux, 1)))
-        c, c_north, z = ys[t] if t < 2 else y_parts(t)
-        s = minmod(c_north - c, c - cpad[t, 6:78])
-        spad[0:72] = s
-        flux = ay * c + by * c_north + py * s + qy * spad[1:73] + vy * z
-        fpad[0:72] = flux
-        write(t, land * (result - (fpad[1:65] - fpad[0:64])))
-
-
-def level_scratch():
-    return [
-        pltpu.VMEM((NTR, 80, LANES), F32),
-        pltpu.VMEM((NTR, 80, LANES), F32),
-        pltpu.VMEM((80, LANES), F32),
-        pltpu.VMEM((80, LANES), F32),
-        pltpu.VMEM((80, LANES), F32),
-        pltpu.VMEM((80, LANES), F32),
-    ]
-
-
-def deep_kernel(first, below, here, above, east, north, mask, west_cols, east_cols, own_cols, row_below, row_above, out, *scratch):
-    k = pl.program_id(0) + first
-    levels = own_cols.shape[0]
-    level = {-1: k - 1, 0: k, 1: jnp.minimum(k + 1, levels - 1)}
-    lane_of_four = lanes_of((8, LANES)) % 4
-    sources = {-1: below, 0: here, 1: above}
-
-    def write(t, value):
-        out[t, 0] = value
-
-    level_step(
-        lambda j, t: sources[j][t, 0],
-        lambda j, i, f: row_below[level[j], i, f : f + 1],
-        lambda j, i, f: row_above[level[j], i, f : f + 1],
-        lambda j, h: jnp.where(lane_of_four < 2, west_cols[level[j], h], east_cols[level[j], h]),
-        lambda j, h: own_cols[level[j], h],
-        east[0],
-        north[0],
-        mask[0].astype(F32),
-        write,
-        scratch,
-    )
+
+def chunk_spans(lo, hi):
+    spans, size = [], 4
+    while lo < hi:
+        end = min(lo + size, hi)
+        if hi - end < size:
+            end = hi
+        spans.append((lo, end))
+        lo, size = end, size + 2
+    return spans
+
+
+def deep_kernel(
+    first, together, tracers, east, north, mask, west_cols, east_cols, own_cols, row_below, row_above, out,
+    cells, flows_e, flows_n, lands, west_v, east_v, own_v, below_v, above_v, results, edges, halo_sem, level_sem, out_sem, *scratch
+):
+    levels = cells.shape[1]
+
+    def halo_copies():
+        pairs = ((row_below, below_v), (row_above, above_v), (west_cols, west_v), (east_cols, east_v), (own_cols, own_v))
+        return [pltpu.make_async_copy(a, b, halo_sem.at[i]) for i, (a, b) in enumerate(pairs)]
+
+    spans = chunk_spans(first - 1, levels)
+    sends = chunk_spans(first, levels)[::-1]
+    sends = [(first + levels - hi, first + levels - lo) for lo, hi in sends]
+
+    def cell_copy(i):
+        lo, hi = spans[i]
+        return pltpu.make_async_copy(tracers.at[:, lo:hi], cells.at[:, lo:hi, 8:72], level_sem.at[0, i])
+
+    def flow_copies(i):
+        lo, hi = spans[i]
+        pairs = ((east, flows_e), (north, flows_n), (mask, lands))
+        return [pltpu.make_async_copy(a.at[lo:hi], b.at[lo:hi], level_sem.at[1 + j, i]) for j, (a, b) in enumerate(pairs)]
+
+    def out_copy(i):
+        lo, hi = sends[i]
+        return pltpu.make_async_copy(results.at[:, lo - first : hi - first], out.at[:, lo:hi], out_sem.at[i])
+
+    cell_copy(0).start()
+    for copy in flow_copies(0) + halo_copies():
+        copy.start()
+    for i in range(1, len(spans)):
+        cell_copy(i).start()
+        for copy in flow_copies(i):
+            copy.start()
+    for copy in halo_copies():
+        copy.wait()
+    for lo in range(first, levels, EDGE_LEVELS):
+        ks = range(lo, min(lo + EDGE_LEVELS, levels))
+        stacked = (8 * len(ks), LANES)
+        lane_of_four = lanes_of(stacked) % 4
+
+        def stack(ref, j, h):
+            return jnp.concatenate([ref[min(k + j, levels - 1), h] for k in ks], 0)
+
+        slopes, fluxes = edge_values(
+            lambda j, h: jnp.where(lane_of_four < 2, stack(west_v, j, h), stack(east_v, j, h)),
+            lambda j, h: stack(own_v, j, h),
+        )
+        for i, k in enumerate(ks):
+            edges[k, 0] = slopes[8 * i : 8 * i + 8]
+            edges[k, 1] = fluxes[8 * i : 8 * i + 8]
+    for copy in flow_copies(0) + [cell_copy(0)]:
+        copy.wait()
+
+    def several(i, _):
+        k0 = first + i * together
+        for i in range(1, len(spans)):
+
+            @pl.when(jnp.logical_and(k0 + together >= spans[i][0], k0 < spans[i][0]))
+            def _():
+                for copy in flow_copies(i) + [cell_copy(i)]:
+                    copy.wait()
+
+        size = len(scratch) // together
+        in_step(*[one(k0 + j, scratch[j * size : (j + 1) * size]) for j in range(together)])
+        for i in range(len(sends)):
+
+            @pl.when(k0 + together == sends[i][1])
+            def _():
+                out_copy(i).start()
+
+        return 0
+
+    def one(k, scratch):
+        level = {-1: k - 1, 0: k, 1: jnp.minimum(k + 1, levels - 1)}
+
+        def write(t, part, value):
+            results[t, k - first, part] = value
+
+        return level_step(
+            cells.at[:, k - 1],
+            cells.at[:, k],
+            cells.at[:, level[1]],
+            lambda j, i: below_v[level[j], i],
+            lambda j, i: above_v[level[j], i],
+            edges[k, 0],
+            edges[k, 1],
+            flows_e[k],
+            flows_n[k],
+            lands[k].astype(F32),
+            write,
+            scratch,
+        )
+
+    lax.fori_loop(0, (levels - first) // together, several, 0)
+    for i in range(len(sends)):
+        out_copy(i).wait()
 
 
 def deep_levels(first, tracers, east, north, mask, west_cols, east_cols, own_cols, row_below, row_above):
     levels = tracers.shape[1]
-    block = (NTR, 1, ROWS, LANES)
-    flow = pl.BlockSpec((1, ROWS, LANES), lambda i: (i + first, 0, 0))
-    whole = lambda x: pl.BlockSpec(x.shape, lambda i: (0,) * x.ndim)
+    halos = (west_cols, east_cols, own_cols, row_below, row_above)
+    flow = (levels, ROWS, LANES)
     return pl.pallas_call(
-        functools.partial(deep_kernel, first),
-        grid=(levels - first,),
-        in_specs=[
-            pl.BlockSpec(block, lambda i: (0, i + first - 1, 0, 0)),
-            pl.BlockSpec(block, lambda i: (0, i + first, 0, 0)),
-            pl.BlockSpec(block, lambda i: (0, jnp.minimum(i + first + 1, levels - 1), 0, 0)),
-            flow,
-            flow,
-            flow,
+        functools.partial(deep_kernel, first, TOGETHER),
+        in_specs=[pl.BlockSpec(memory_space=pl.ANY)] * 9,
+        out_specs=pl.BlockSpec(memory_space=pl.ANY),
+        out_shape=jax.ShapeDtypeStruct(tracers.shape, F32),
+        scratch_shapes=[
+            pltpu.VMEM((NTR, levels, ROWS + 16, LANES), F32),
+            pltpu.VMEM(flow, F32),
+            pltpu.VMEM(flow, F32),
+            pltpu.VMEM(flow, jnp.int32),
         ]
-        + [whole(x) for x in (west_cols, east_cols, own_cols, row_below, row_above)],
-        out_specs=pl.BlockSpec(block, lambda i: (0, i + first, 0, 0)),
-        out_shape=jax.ShapeDtypeStruct(tracers.shape, F32),
-        scratch_shapes=level_scratch(),
-        compiler_params=pltpu.CompilerParams(vmem_limit_bytes=VMEM_LIMIT),
+        + [pltpu.VMEM(x.shape, F32) for x in halos]
+        + [
+            pltpu.VMEM((NTR, levels - first, ROWS, LANES), F32),
+            pltpu.VMEM((levels, 2, 8, LANES), F32),
+            pltpu.SemaphoreType.DMA((5,)),
+            pltpu.SemaphoreType.DMA((4, levels)),
+            pltpu.SemaphoreType.DMA((levels,)),
+        ]
+        + level_scratch() * TOGETHER,
+        compiler_params=pltpu.CompilerParams(vmem_limit_bytes=24 * 1024 * 1024),
         name="deep_levels",
-    )(tracers, tracers, tracers, east, north, mask, west_cols, east_cols, own_cols, row_below, row_above)
+    )(tracers, east, north, mask, *halos)
 
 
 def expand(x, lane):
@@ -400,8 +560,10 @@
 
 def surface_kernel(
     top, arrived, tracers, east, north, mask, west_cols, east_cols, own_cols, row_below, row_above, _, forcing, out,
-    forced, rows_b, rows_a, cols_h, cols_o, *scratch
+    cells, cell_sem, rows_b, rows_a, cols_h, cols_o, *scratch
 ):
+    copy = pltpu.make_async_copy(tracers.at[:, 0:3], cells.at[:, :, 8:72], cell_sem)
+    copy.start()
     devices = arrived.shape[0] // (4 * GROUPS)
     stride = 4 * GROUPS
     lane = lanes_of((8, LANES))
@@ -439,18 +601,16 @@
             lined = jnp.where((wide < 12) & (wide % 4 // 2 == side), lined, 0.0)
             beside += dot(pick(4 + 4 * side + n), lined)
 
-    def summed(group):
-        return jnp.sum(arrived[...].reshape(devices, GROUPS, 4, LANES)[:, group], 0)
-
     over = [jnp.sum(gathered(6, f), 0, keepdims=True) for f in range(4)]
     under = [jnp.sum(gathered(7, f), 0, keepdims=True) for f in range(4)]
     tau_under = jnp.sum(gathered(4, 1), 0, keepdims=True)
 
     land = [mask[k].astype(F32) for k in range(2)]
-    forced[0] = tracers[0, 0] + land[0] * (HEAT_SCALE * heat)
+    copy.wait()
+    cells[0, 0, 8:72] = cells[0, 0, 8:72] + land[0] * (HEAT_SCALE * heat)
     for t in range(1, NTR):
-        c = tracers[t, 0]
-        forced[t] = c + land[0] * (FRESH_SCALE * fresh * c)
+        c = cells[t, 0, 8:72]
+        cells[t, 0, 8:72] = c + land[0] * (FRESH_SCALE * fresh * c)
     rows_b[0] = force_rows(row_below[0, 0], row_below[0, 0, 7:8], under[2], under[3], 0.0)
     rows_b[1] = force_rows(row_below[0, 1], row_below[0, 1, 7:8], under[0], under[1], tau_under)
     near = jnp.where(top[0] > 0, row_above[0, 1, 7:8], row_above[0, 0, 7:8])
@@ -468,29 +628,40 @@
         cols_h[h] = force_columns(cols, halo_force[h], lane)
         cols_o[h] = force_columns(own_cols[0, h], own_force[h], lane)
 
-    for k in range(2):
-
+    def level(k):
         def at(j):
             return max(k + j, 0)
 
-        def write(t, value):
-            out[t, k] = value
-
-        def plain_halo(level, h):
-            return jnp.where(lane_of_four < 2, west_cols[level, h], east_cols[level, h])
-
-        level_step(
-            lambda j, t: forced[t] if at(j) == 0 else tracers[t, at(j)],
-            lambda j, i, f: rows_b[i, f : f + 1] if at(j) == 0 else row_below[at(j), i, f : f + 1],
-            lambda j, i, f: rows_a[i, f : f + 1] if at(j) == 0 else row_above[at(j), i, f : f + 1],
-            lambda j, h: cols_h[h] if at(j) == 0 else plain_halo(at(j), h),
-            lambda j, h: cols_o[h] if at(j) == 0 else own_cols[at(j), h],
+        def write(t, part, value):
+            out[t, k, part] = value
+
+        size = len(scratch) // 2
+        return level_step(
+            cells.at[:, at(-1)],
+            cells.at[:, k],
+            cells.at[:, k + 1],
+            lambda j, i: rows_b[i] if at(j) == 0 else row_below[at(j), i],
+            lambda j, i: rows_a[i] if at(j) == 0 else row_above[at(j), i],
+            slopes[8 * k : 8 * k + 8],
+            fluxes[8 * k : 8 * k + 8],
             east[k] + STRESS_SCALE * tau_x if k == 0 else east[k],
             north[k] + STRESS_SCALE * tau_y if k == 0 else north[k],
             land[k],
             write,
-            scratch,
+            scratch[size * k : size * (k + 1)],
         )
+
+    def halo_at(k, h):
+        return cols_h[h] if k <= 0 else jnp.where(lane_of_four < 2, west_cols[k, h], east_cols[k, h])
+
+    def own_at(k, h):
+        return cols_o[h] if k <= 0 else own_cols[k, h]
+
+    slopes, fluxes = edge_values(
+        lambda j, h: jnp.concatenate([halo_at(k + j, h) for k in range(2)], 0),
+        lambda j, h: jnp.concatenate([own_at(k + j, h) for k in range(2)], 0),
+    )
+    in_step(level(0), level(1))
 
 
 def surface_levels(top, arrived, tracers, east, north, mask, west_cols, east_cols, own_cols, row_below, row_above, done):
@@ -503,7 +674,7 @@
         in_specs=[
             pl.BlockSpec(memory_space=pltpu.SMEM),
             pl.BlockSpec(arrived.shape, lambda i: (0, 0)),
-            block(3),
+            pl.BlockSpec(memory_space=pl.ANY),
             flow,
             flow,
             flow,
@@ -514,13 +685,14 @@
         out_shape=[jax.ShapeDtypeStruct((4, ROWS, LANES), F32), jax.ShapeDtypeStruct(tracers.shape, F32)],
         input_output_aliases={11: 1},
         scratch_shapes=[
-            pltpu.VMEM((NTR, ROWS, LANES), F32),
+            pltpu.VMEM((NTR, 3, ROWS + 16, LANES), F32),
+            pltpu.SemaphoreType.DMA,
             pltpu.VMEM((2, 8, LANES), F32),
             pltpu.VMEM((2, 8, LANES), F32),
             pltpu.VMEM((2, 8, LANES), F32),
             pltpu.VMEM((2, 8, LANES), F32),
         ]
-        + level_scratch(),
+        + level_scratch() * 2,
         compiler_params=pltpu.CompilerParams(vmem_limit_bytes=VMEM_LIMIT),
         name="surface_levels",
     )(top, arrived, tracers, east, north, mask, west_cols, east_cols, own_cols, row_below, row_above, done)
@@ -546,11 +718,6 @@
     lon, lat = lax.axis_index("lon"), lax.axis_index("lat")
     columns = n_lon * LANES
     c = (fold_partner[0] + lon * LANES) % columns
-
-    outgoing = remap(atm_fields, remap_weights, remap_src, remap_dst, c[None], n_lon, n_lat)
-    arrived = lax.all_to_all(
-        outgoing.reshape(devices, 4 * GROUPS, LANES), ("lon", "lat"), split_axis=0, concat_axis=0, tiled=True
-    )
 
     both, own_cols, up, down = pack_halos(tracers, flow_east, flow_north, sea_mask)
     right = [(i, (i + 1) % n_lon) for i in range(n_lon)]
@@ -561,7 +728,16 @@
     east_cols = lax.ppermute(own_cols, "lon", left)
     row_below = lax.ppermute(up, "lat", north)
     row_above = lax.ppermute(down, "lat", south)
+    atm_fields, _ = lax.optimization_barrier((atm_fields, both))
+    outgoing = remap(atm_fields, remap_weights, remap_src, remap_dst, c[None], n_lon, n_lat)
+    west_cols, outgoing = lax.optimization_barrier((west_cols, outgoing))
     ghost = fold_ghost(both[:, 2], west_cols[:, 2], c, n_lon, n_lat)
+    outgoing, ghost, east_cols, row_below, row_above = lax.optimization_barrier(
+        (outgoing, ghost, east_cols, row_below, row_above)
+    )
+    arrived = lax.all_to_all(
+        outgoing.reshape(devices, 4 * GROUPS, LANES), ("lon", "lat"), split_axis=0, concat_axis=0, tiled=True
+    )
     is_top = lat == n_lat - 1
     field = jnp.arange(8)[:, None]
     ghost_rows = jnp.stack([jnp.where(field == 7, 1.0, ghost), ghost], 1)

time: 110 us -> 87.1 us (0.79)
  the two profiles are of different devices: /device:TPU:2 before, /device:TPU:0 now
where the time goes in v1:
time: 87.1 us; the launch traced here: 86.9 us
  Pallas kernels  43.3 us (50%)
  starting transfers between devices  29.8 us (34%)
  waiting for transfers between devices  7.24 us (8%)
  local copies, waits for them, and re-layouts  2.37 us (3%)
  other arithmetic  2.02 us (2%)
  matrix products  1.24 us (1%)
  between operations  0.94 us (1%)
    pallas_call x1, Pallas kernels, deep_levels(): pl.pallas_call(functools.partial(deep_kernel, first, TOGETHER), in_specs=...  18.3 us
    all_to_all x1, starting transfers between devices, body(): lax.all_to_all(outgoing.reshape(devices, 4 * GROUPS, LANES), ('lon', 'lat...  18.1 us
    pallas_call x1, Pallas kernels, remap(): pl.pallas_call(functools.partial(remap_kernel, n_lon, n_lat, per_step), g...  12.5 us
    all_to_all x1, waiting for transfers between devices, body(): lax.all_to_all(outgoing.reshape(devices, 4 * GROUPS, LANES), ('lon', 'lat...  7.23 us
    pallas_call x1, Pallas kernels, surface_levels(): pl.pallas_call(surface_kernel, grid=(1,), in_specs=[pl.BlockSpec(memory_s...  6.26 us
    pallas_call x1, Pallas kernels, pack_halos(): pl.pallas_call(pack_kernel, grid=(levels // step,), in_specs=[pl.BlockSpe...  6.26 us
    ppermute x1, starting transfers between devices, body(): east_cols = lax.ppermute(own_cols, 'lon', left)  5.12 us
    ppermute x1, starting transfers between devices, body(): row_below = lax.ppermute(up, 'lat', north)  3.92 us
  transfers between devices with their start and end apart: 6, of which 1 were waited for; matrix products, arithmetic and copies ran while one was open for 4% of the time, Pallas kernels for 35%

profile of v1, /device:TPU:0, one launch (start us, length us, event | category | flops | bytes accessed | tf_op | source)
XLA Modules:
  0.0 86.9 jit_solution(810987673141021933)
XLA Ops:
  0.6 6.3 %pack_halos.1 = (f32[24,3,8,128]{3,2,1,0:T(8,128)}, f32[24,2,8,128]{3,2,1,0:T(8,128)}, f32[24,2,8,128]{3,2,1,0:T(8,128)}, f32[24,2,8,128]{3,2,1,0:T(8,128)}) custom-call(f32[6,24,64,128]{3,2,1,0:T(8,128)} %tracers.5, f32[24,64,128]{2,1,0:T(8,128)} %east.5, f32[24,64,128]{2,1,0:T(8,128)} %north.5, s32[24,64,128]{2,1,0:T(8,128)} %mask.5), custom_call_target="tpu_custom_call" | custom-call | tf_op jit(solution)/shard_map/pack_halos/pallas_call | solution.py:76
  6.9 0.0 collective-permute-start.16
  6.9 3.9 %collective-permute-start.18 = (f32[24,2,8,128]{3,2,1,0:T(8,128)}, f32[24,2,8,128]{3,2,1,0:T(8,128)S(1)}, u32[]{:S(2)}, u32[]{:S(2)}) collective-permute-start(f32[24,2,8,128]{3,2,1,0:T(8,128)} %get-tuple-element.52), channel_id=1, source_target_pairs={{0,1},{1,2},{2,3},{3,4},{4,5},{5,6},{6,7},{8,9},{9,10},{10,11},{11... | collective-permute-start | bytes 589832 | tf_op jit(solution)/shard_map/ppermute | solution.py:729
  10.9 1.3 %collective-permute-start.19 = (f32[24,2,8,128]{3,2,1,0:T(8,128)}, f32[24,2,8,128]{3,2,1,0:T(8,128)S(1)}, u32[]{:S(2)}, u32[]{:S(2)}) collective-permute-start(f32[24,2,8,128]{3,2,1,0:T(8,128)} %get-tuple-element.53), channel_id=1, source_target_pairs={{1,0},{2,1},{3,2},{4,3},{5,4},{6,5},{7,6},{9,8},{10,9},{11,10},{12... | collective-permute-start | bytes 589832 | tf_op jit(solution)/shard_map/ppermute | solution.py:730
  12.2 5.1 %collective-permute-start.17 = (f32[24,2,8,128]{3,2,1,0:T(8,128)}, f32[24,2,8,128]{3,2,1,0:T(8,128)S(1)}, u32[]{:S(2)}, u32[]{:S(2)}) collective-permute-start(f32[24,2,8,128]{3,2,1,0:T(8,128)} %get-tuple-element.51.own_cols), channel_id=1, source_target_pairs={{8,0},{16,8},{24,16},{32,24},{40,32},{48,40},{56,48},{64,56},{72,6... | collective-permute-start | bytes 589832 | tf_op jit(solution)/shard_map/ppermute | solution.py:728
  17.4 12.5 %remap.1 = f32[1024,4,128]{2,1,0:T(4,128)} custom-call(s32[256]{0:T(256)} %src.1, s32[256]{0:T(256)} %dst.1, s32[1]{0:T(128)} %bitcast.2.fold, bf16[4,8192]{1,0:T(4,128)(2,1)} %atm, bf16[256,128,128]{2,1,0:T(8,128)(2,1)} %weights.1), custom_call_target="tpu_custom_call" | custom-call | tf_op jit(solution)/shard_map/remap/pallas_call | solution.py:194
  29.9 0.0 collective-permute-done.16.west_cols
  30.0 1.2 %fusion.1 = f32[24,8,128]{2,1,0:T(8,128)S(1)} fusion(f32[24,3,8,128]{3,2,1,0:T(8,128)S(1)} %collective-permute-done.16.west_cols, pred[128]{0:T(512)(128)(4,1)S(1)} %iota_compare_fusion.2, s32[128]{0:T(128)S(1)} %and_select_fusion, f32[24,3,8,128]{3,2,1,0:T(8,128)} %get-tuple-element.47), kind=kOutput, calls=%fused_computation.3 | convolution fusion | flops 37789696 | bytes 295936 | tf_op jit(solution)/shard_map/kfl,li->kfi/dot_general | solution.py:706
  31.2 1.3 %conditional.1 = (f32[24,8,128]{2,1,0:T(8,128)}) conditional(s32[]{:T(128)} %clamp.3, f32[24,8,128]{2,1,0:T(8,128)S(1)} %fusion.1, f32[24,8,128]{2,1,0:T(8,128)S(1)} %fusion.1, f32[24,8,128]{2,1,0:T(8,128)S(1)} %fusion.1, f32[24,8,128]{2,1,0:T(8,128)S(1)} %fusion.1, f32[24,8,128]{2,1,0:T(8,128)S(1)} %fusion.1, ...), branch_computations={%region_0.1_spmd, %region_1.2_spmd, %region_2.3_spmd, %region_3.4_... | conditional | bytes 393264 | solution.py:712
  31.2 1.3 %collective-permute-start.3 = (f32[24,8,128]{2,1,0:T(8,128)S(1)}, f32[24,8,128]{2,1,0:T(8,128)}, u32[]{:S(2)}, u32[]{:S(2)}) collective-permute-start(f32[24,8,128]{2,1,0:T(8,128)S(1)} %param.3), channel_id=1, source_target_pairs={{7,31},{15,23},{23,15},{31,7},{39,127},{47,119},{55,111},{63,103},... | collective-permute-start | bytes 294920 | tf_op jit(solution)/shard_map/cond/branch_3_fun/ppermute | solution.py:710
  32.5 0.0 collective-permute-done.3
  32.6 0.0 collective-permute-done.18.row_below
  32.6 0.0 collective-permute-done.19
  32.6 0.0 copy-start.9
  32.6 0.0 collective-permute-done.17.east_cols
  32.6 18.1 %all-to-all-start = ((f32[128,32,128]{2,1,0:T(8,128)}), f32[128,32,128]{2,1,0:T(8,128)}, u32[]{:S(2)}, u32[]{:S(2)}) async-start(f32[128,32,128]{2,1,0:T(8,128)} %bitcast.22), calls=%async_computation | async-start | bytes 4194304 | tf_op jit(solution)/shard_map/all_to_all | solution.py:738
  50.7 1.0 %select_bitcast_fusion = f32[24,1,8,128]{3,2,1,0:T(8,128)S(1)} fusion(f32[24,8,128]{2,1,0:T(8,128)} %get-tuple-element.59, pred[8]{0:T(512)(128)(4,1)S(1)} %iota_compare_fusion.1), kind=kLoop, calls=%fused_computation.5 | loop fusion | flops 24576 | bytes 196616 | tf_op jit(solution)/shard_map/stack | solution.py:743
  51.7 1.0 %maximum_select_fusion.row_above = f32[24,2,8,128]{3,2,1,0:T(8,128)S(1)} fusion(f32[24,2,8,128]{3,2,1,0:T(8,128)} %copy-done.9, f32[24,1,8,128]{3,2,1,0:T(8,128)} %bitcast.9, f32[24,1,8,128]{3,2,1,0:T(8,128)S(1)} %select_bitcast_fusion, pred[]{:T(512)S(6)} %eq.27), kind=kLoop, calls=%fused_computation | loop fusion | flops 98304 | bytes 589825 | tf_op jit(solution)/shard_map/jit(_where)/select_n | solution.py:744
  52.8 0.0 copy-start
  52.8 2.3 %copy-done = f32[6,24,64,128]{3,2,1,0:T(8,128)S(1)} copy-done((f32[6,24,64,128]{3,2,1,0:T(8,128)S(1)}, f32[6,24,64,128]{3,2,1,0:T(8,128)}, u32[]{:S(2)}) %copy-start) | copy-done | bytes 4718616
  55.1 18.3 %deep_levels.1._ = f32[6,24,64,128]{3,2,1,0:T(8,128)} custom-call(f32[6,24,64,128]{3,2,1,0:T(8,128)S(1)} %copy-done, f32[24,64,128]{2,1,0:T(8,128)S(1)} %copy-done.1, f32[24,64,128]{2,1,0:T(8,128)S(1)} %copy-done.2, s32[24,64,128]{2,1,0:T(8,128)S(1)} %copy-done.3, f32[24,3,8,128]{3,2,1,0:T(8,128)S(1)} %collective-permute-done.16.west_cols, ...), custom_call_target="tpu_custom_call" | custom-call | tf_op jit(solution)/shard_map/deep_levels/pallas_call | solution.py:506
  73.4 0.0 copy-done.5
  73.4 7.2 %all-to-all-done = f32[128,32,128]{2,1,0:T(8,128)} async-done(((f32[128,32,128]{2,1,0:T(8,128)}), f32[128,32,128]{2,1,0:T(8,128)}, u32[]{:S(2)}, u32[]{:S(2)}) %all-to-all-start) | async-done | bytes 2097184 | tf_op jit(solution)/shard_map/all_to_all | solution.py:738
  80.7 6.3 %surface_levels.1 = (f32[4,64,128]{2,1,0:T(8,128)}, f32[6,24,64,128]{3,2,1,0:T(8,128)}) custom-call(s32[1]{0:T(128)} %bitcast.top, f32[4096,128]{1,0:T(8,128)} %bitcast.7.arrived, f32[6,24,64,128]{3,2,1,0:T(8,128)} %tracers.5, f32[24,64,128]{2,1,0:T(8,128)} %east.5, f32[24,64,128]{2,1,0:T(8,128)} %north.5, ...), custom_call_target="tpu_custom_call", output_to_operand_aliasing={{1}: (11, {})} | custom-call | tf_op jit(solution)/shard_map/surface_levels/pallas_call | solution.py:671
  (21 shorter events, 0.1 us)
Async XLA Ops:
  0.6 16.7 %copy-start.10 = (s32[128]{0:T(128)S(1)}, s32[128]{0:T(128)}, u32[]{:S(2)}) copy-start(s32[128]{0:T(128)} %param.33) | copy-start | bytes 1540
  6.9 23.0 %collective-permute-start.16 = (f32[24,3,8,128]{3,2,1,0:T(8,128)}, f32[24,3,8,128]{3,2,1,0:T(8,128)S(1)}, u32[]{:S(2)}, u32[]{:S(2)}) collective-permute-start(f32[24,3,8,128]{3,2,1,0:T(8,128)} %get-tuple-element.47), channel_id=1, source_target_pairs={{0,8},{8,16},{16,24},{24,32},{32,40},{40,48},{48,56},{56,64},{64,7... | collective-permute-start | bytes 884744 | tf_op jit(solution)/shard_map/ppermute | solution.py:727
  6.9 25.6 %collective-permute-start.18 = (f32[24,2,8,128]{3,2,1,0:T(8,128)}, f32[24,2,8,128]{3,2,1,0:T(8,128)S(1)}, u32[]{:S(2)}, u32[]{:S(2)}) collective-permute-start(f32[24,2,8,128]{3,2,1,0:T(8,128)} %get-tuple-element.52), channel_id=1, source_target_pairs={{0,1},{1,2},{2,3},{3,4},{4,5},{5,6},{6,7},{8,9},{9,10},{10,11},{11... | collective-permute-start | bytes 589832 | tf_op jit(solution)/shard_map/ppermute | solution.py:729
  10.9 21.7 %collective-permute-start.19 = (f32[24,2,8,128]{3,2,1,0:T(8,128)}, f32[24,2,8,128]{3,2,1,0:T(8,128)S(1)}, u32[]{:S(2)}, u32[]{:S(2)}) collective-permute-start(f32[24,2,8,128]{3,2,1,0:T(8,128)} %get-tuple-element.53), channel_id=1, source_target_pairs={{1,0},{2,1},{3,2},{4,3},{5,4},{6,5},{7,6},{9,8},{10,9},{11,10},{12... | collective-permute-start | bytes 589832 | tf_op jit(solution)/shard_map/ppermute | solution.py:730
  12.2 20.4 %collective-permute-start.17 = (f32[24,2,8,128]{3,2,1,0:T(8,128)}, f32[24,2,8,128]{3,2,1,0:T(8,128)S(1)}, u32[]{:S(2)}, u32[]{:S(2)}) collective-permute-start(f32[24,2,8,128]{3,2,1,0:T(8,128)} %get-tuple-element.51.own_cols), channel_id=1, source_target_pairs={{8,0},{16,8},{24,16},{32,24},{40,32},{48,40},{56,48},{64,56},{72,6... | collective-permute-start | bytes 589832 | tf_op jit(solution)/shard_map/ppermute | solution.py:728
  29.9 22.9 %copy-start.1 = (f32[24,64,128]{2,1,0:T(8,128)S(1)}, f32[24,64,128]{2,1,0:T(8,128)}, u32[]{:S(2)}) copy-start(f32[24,64,128]{2,1,0:T(8,128)} %east.5) | copy-start | bytes 2359300
  29.9 22.9 %copy-start.2 = (f32[24,64,128]{2,1,0:T(8,128)S(1)}, f32[24,64,128]{2,1,0:T(8,128)}, u32[]{:S(2)}) copy-start(f32[24,64,128]{2,1,0:T(8,128)} %north.5) | copy-start | bytes 2359300
  29.9 22.9 %copy-start.3 = (s32[24,64,128]{2,1,0:T(8,128)S(1)}, s32[24,64,128]{2,1,0:T(8,128)}, u32[]{:S(2)}) copy-start(s32[24,64,128]{2,1,0:T(8,128)} %mask.5) | copy-start | bytes 2359300
  29.9 22.9 %copy-start.6 = (f32[24,2,8,128]{3,2,1,0:T(8,128)S(1)}, f32[24,2,8,128]{3,2,1,0:T(8,128)}, u32[]{:S(2)}) copy-start(f32[24,2,8,128]{3,2,1,0:T(8,128)} %get-tuple-element.51.own_cols) | copy-start | bytes 589828
  30.0 43.4 %copy-start.5 = (f32[24,3,8,128]{3,2,1,0:T(8,128)}, f32[24,3,8,128]{3,2,1,0:T(8,128)S(1)}, u32[]{:S(2)}) copy-start(f32[24,3,8,128]{3,2,1,0:T(8,128)S(1)} %collective-permute-done.16.west_cols) | copy-start | bytes 884740
  31.2 1.3 %collective-permute-start.3 = (f32[24,8,128]{2,1,0:T(8,128)S(1)}, f32[24,8,128]{2,1,0:T(8,128)}, u32[]{:S(2)}, u32[]{:S(2)}) collective-permute-start(f32[24,8,128]{2,1,0:T(8,128)S(1)} %param.3), channel_id=1, source_target_pairs={{7,31},{15,23},{23,15},{31,7},{39,127},{47,119},{55,111},{63,103},... | collective-permute-start | bytes 294920 | tf_op jit(solution)/shard_map/cond/branch_3_fun/ppermute | solution.py:710
  32.6 40.8 %copy-start.7 = (f32[24,2,8,128]{3,2,1,0:T(8,128)}, f32[24,2,8,128]{3,2,1,0:T(8,128)S(1)}, u32[]{:S(2)}) copy-start(f32[24,2,8,128]{3,2,1,0:T(8,128)S(1)} %collective-permute-done.18.row_below) | copy-start | bytes 589828
  32.6 19.1 %copy-start.9 = (f32[24,2,8,128]{3,2,1,0:T(8,128)}, f32[24,2,8,128]{3,2,1,0:T(8,128)S(1)}, u32[]{:S(2)}) copy-start(f32[24,2,8,128]{3,2,1,0:T(8,128)S(1)} %collective-permute-done.19) | copy-start | bytes 589828
  32.6 40.8 %copy-start.8 = (f32[24,2,8,128]{3,2,1,0:T(8,128)}, f32[24,2,8,128]{3,2,1,0:T(8,128)S(1)}, u32[]{:S(2)}) copy-start(f32[24,2,8,128]{3,2,1,0:T(8,128)S(1)} %collective-permute-done.17.east_cols) | copy-start | bytes 589828
  32.6 48.1 %all-to-all-start = ((f32[128,32,128]{2,1,0:T(8,128)}), f32[128,32,128]{2,1,0:T(8,128)}, u32[]{:S(2)}, u32[]{:S(2)}) async-start(f32[128,32,128]{2,1,0:T(8,128)} %bitcast.22), calls=%async_computation | async-start | bytes 4194304 | tf_op jit(solution)/shard_map/all_to_all | solution.py:738
  52.8 2.3 %copy-start = (f32[6,24,64,128]{3,2,1,0:T(8,128)S(1)}, f32[6,24,64,128]{3,2,1,0:T(8,128)}, u32[]{:S(2)}) copy-start(f32[6,24,64,128]{3,2,1,0:T(8,128)} %tracers.5) | copy-start | bytes 14155780
  55.1 18.3 %copy-start.4 = (f32[24,2,8,128]{3,2,1,0:T(8,128)}, f32[24,2,8,128]{3,2,1,0:T(8,128)S(1)}, u32[]{:S(2)}) copy-start(f32[24,2,8,128]{3,2,1,0:T(8,128)S(1)} %maximum_select_fusion.row_above) | copy-start | bytes 589828
